TPU v7x, 512 devices: a whole 4x4x16 slice. The times are simulated.
512 devices in a mesh: wide: 64 (over y_hi, z, core), narrow: 8 (over x, y_lo).
Axes of the slice: x: 4, y: 4 (y_hi: 2, y_lo: 2; y = y_hi * 2 + y_lo), z: 16, core: 2. Of those that a mesh axis runs over, the one named last changes fastest.
Arguments:
- examples: bfloat16 [320, 8192], P('wide', 'narrow'), may hold values from -6 to 6
- references: bfloat16 [128, 8192], P('wide', 'narrow'), may hold values from -6 to 6
- gate_weight: bfloat16 [8192, 28672], P('narrow', 'wide'), may hold values from -0.0625 to 0.0625
- up_weight: bfloat16 [8192, 28672], P('narrow', 'wide'), may hold values from -0.0625 to 0.0625
- down_weight: bfloat16 [28672, 8192], P('wide', 'narrow'), may hold values from -0.03125 to 0.03125
- cotangent: bfloat16 [320, 8192], P('wide', 'narrow'), may hold values from -6 to 6
- pair_ref: int32 [320, 4], replicated, may hold values from 0 to 127
- points: int32 [8], replicated, may hold values from 1 to 8
Outputs:
- expected: bfloat16 [320, 8192], P('wide', 'narrow')
All inputs are finite; a program needn't handle non-finite values.
Results may differ from a plain program's by a relative error of at most 0.005.
Values may be sent and summed in bfloat16 or wider, within the bound.
A program may use at most 64 MiB of HBM per device.

v0:
```python
import jax
import jax.numpy as jnp
from jax import lax
from jax.sharding import Mesh
from jax.sharding import PartitionSpec as P

WIDE = ("wide_0", "wide_1", "wide_2")


def copy_for_each(x, axis):
    size = lax.axis_size(axis)
    return lax.all_to_all(jnp.broadcast_to(x[None], (size, *x.shape)), axis, 0, 0, tiled=True)


def in_order(blocks, dim):
    blocks = jnp.moveaxis(blocks, 0, dim)
    dims = blocks.shape
    return blocks.reshape(*dims[:dim], dims[dim] * dims[dim + 1], *dims[dim + 2 :])


def gather_axes(x, axes, dim):
    far, near = axes
    blocks = copy_for_each(copy_for_each(x, far), near)
    return in_order(blocks.swapaxes(0, 1).reshape(-1, *x.shape), dim)


def cut_along(x, dim, size):
    before, after = (x.shape[:dim], x.shape[dim + 1 :])
    return jnp.moveaxis(x.reshape(*before, size, -1, *after), dim, 0)


def summed_on_arrival(x, axis, dim):
    blocks = cut_along(x, dim, lax.axis_size(axis))
    arrived = lax.all_to_all(blocks, axis, split_axis=0, concat_axis=0, tiled=True)
    return arrived.sum(axis=0)


def sent_together(arrays, axis, dim, along):
    both = jnp.concatenate(arrays, axis=along)
    out, at, outs = (summed_on_arrival(both, axis, dim), 0, [])
    for a in arrays:
        outs.append(lax.slice_in_dim(out, at, at + a.shape[along], axis=along))
        at += a.shape[along]
    return tuple(outs)


def turned_gather(arrays, axis, dims):
    turned = [jnp.moveaxis(a, dim, 0) for a, dim in zip(arrays, dims)]
    widths = [t[0].size for t in turned]
    both = jnp.concatenate([t.reshape(-1, w) for t, w in zip(turned, widths)], axis=1)
    out = lax.all_gather(both, axis, axis=0, tiled=True)
    blocks = jnp.split(out, [sum(widths[:k]) for k in range(1, len(widths))], axis=1)
    return tuple(
        (
            jnp.moveaxis(b.reshape(-1, *t.shape[1:]), 0, dim)
            for b, t, dim in zip(blocks, turned, dims)
        )
    )


def sum_in_two_steps(x, axes, dim):
    far, near = axes
    own = summed_on_arrival(cut_along(x, dim, lax.axis_size(far)), near, dim + 1)
    return jnp.sum(lax.all_to_all(own, far, 0, 0, tiled=True), axis=0)


def path_coefficients(example_gate, example_up, reference_gate, reference_up, pair_ref, points):
    alphas = points.astype(jnp.float32) / 8.0
    coef_gate = jnp.zeros(example_gate.shape, jnp.float32)
    coef_up = jnp.zeros(example_gate.shape, jnp.float32)
    for pair_slot in range(pair_ref.shape[1]):
        chosen = pair_ref[:, pair_slot]
        base_gate = jnp.take(reference_gate, chosen, axis=0)
        base_up = jnp.take(reference_up, chosen, axis=0)
        step_gate = example_gate - base_gate
        step_up = example_up - base_up
        for point_slot in range(alphas.shape[0]):
            position = alphas[point_slot]
            along_gate = base_gate + position * step_gate
            along_up = base_up + position * step_up
            sigmoid = jax.nn.sigmoid(along_gate)
            coef_gate = coef_gate + along_up * sigmoid * (1.0 + along_gate * (1.0 - sigmoid))
            coef_up = coef_up + along_gate * sigmoid
    total = pair_ref.shape[1] * alphas.shape[0]
    return (coef_gate / total, coef_up / total)


def transposed_product(left, right):
    return lax.dot_general(
        left, right, (((1,), (1,)), ((), ())), preferred_element_type=jnp.float32
    )


def on_device(
    examples, references, gate_weight, up_weight, down_weight, cotangent, pair_ref, points
):
    all_examples, all_references, all_cotangent = (
        gather_axes(examples, (("wide_0", "wide_1"), "wide_2"), 0),
        gather_axes(references, (("wide_0", "wide_1"), "wide_2"), 0),
        gather_axes(cotangent, (("wide_0", "wide_1"), "wide_2"), 0),
    )
    gate_terms = jnp.dot(all_examples, gate_weight, preferred_element_type=jnp.float32)
    up_terms = jnp.dot(all_examples, up_weight, preferred_element_type=jnp.float32)
    reference_gate_terms = jnp.dot(all_references, gate_weight, preferred_element_type=jnp.float32)
    reference_up_terms = jnp.dot(all_references, up_weight, preferred_element_type=jnp.float32)
    upstream_terms = transposed_product(all_cotangent, down_weight)
    example_gate, example_up, reference_gate, reference_up, upstream = sent_together(
        (gate_terms, up_terms, reference_gate_terms, reference_up_terms, upstream_terms),
        "narrow",
        1,
        0,
    )
    coef_gate, coef_up = path_coefficients(
        example_gate, example_up, reference_gate, reference_up, pair_ref, points
    )
    grad_gate = (upstream * coef_gate).astype(jnp.bfloat16)
    grad_up = (upstream * coef_up).astype(jnp.bfloat16)
    full_gate, full_up = turned_gather((grad_gate, grad_up), "narrow", (1, 1))
    result = sum_in_two_steps(
        transposed_product(full_gate, gate_weight) + transposed_product(full_up, up_weight),
        (("wide_0", "wide_1"), "wide_2"),
        0,
    )
    return result.astype(jnp.bfloat16)


def solution(mesh):
    split = Mesh(
        mesh.devices.reshape(2, 16, 2, mesh.shape["narrow"]),
        ("wide_0", "wide_1", "wide_2", "narrow"),
    )
    placed = (
        P(WIDE, "narrow"),
        P(WIDE, "narrow"),
        P("narrow", WIDE),
        P("narrow", WIDE),
        P(WIDE, "narrow"),
        P(WIDE, "narrow"),
        P(),
        P(),
    )
    return jax.shard_map(
        on_device, mesh=split, in_specs=placed, out_specs=P(WIDE, "narrow"), check_vma=False
    )
```

profile of v0, /device:TPU:32, one launch (start us, length us, event | category | flops | bytes accessed | tf_op | source)
XLA Modules:
  0.0 296.1 jit_solution(9119121526575013563)
XLA Ops:
  0.0 0.8 broadcast_in_dim.20
  0.8 35.1 %all_to_all.45 = bf16[32,2,1024]{2,1,0:T(2,128)(2,1)S(1)} all-to-all(bf16[32,2,1024]{2,1,0:T(2,128)(2,1)S(1)} %broadcast_in_dim.20), channel_id=1, replica_groups=mesh['wide_0'=2,'wide_1'=16,'wide_2'=2,'narrow'=8] {'wide_0','wide_1'}, dimensions={0} | all-to-all | bytes 262144 | tf_op jit(solution)/shard_map/all_to_all | solution.py:12
  36.0 0.8 broadcast_in_dim.18
  36.8 37.0 %all_to_all.46 = bf16[32,5,1024]{2,1,0:T(8,128)(2,1)S(1)} all-to-all(bf16[32,5,1024]{2,1,0:T(8,128)(2,1)S(1)} %broadcast_in_dim.18), channel_id=1, replica_groups=mesh['wide_0'=2,'wide_1'=16,'wide_2'=2,'narrow'=8] {'wide_0','wide_1'}, dimensions={0} | all-to-all | bytes 655360 | tf_op jit(solution)/shard_map/all_to_all | solution.py:12
  73.7 0.8 broadcast_in_dim.21
  74.6 3.4 %all-to-all-start.3 = ((bf16[2,32,2,1024]{3,2,1,0:T(2,128)(2,1)}), bf16[2,32,2,1024]{3,2,1,0:T(2,128)(2,1)S(1)}, u32[]{:S(2)}, u32[]{:S(2)}) async-start(bf16[2,32,2,1024]{3,2,1,0:T(2,128)(2,1)} %broadcast_in_dim.21), calls=%async_computation.3 | async-start | bytes 524288 | tf_op jit(solution)/shard_map/all_to_all | solution.py:12
  78.0 0.2 copy.61
  78.2 1.3 all-to-all-done.3
  79.5 0.1 broadcast_in_dim.19
  79.6 4.3 %all_to_all.47 = bf16[2,32,5,1024]{3,1,2,0:T(8,128)(2,1)S(1)} all-to-all(bf16[2,32,5,1024]{3,1,2,0:T(8,128)(2,1)S(1)} %broadcast_in_dim.19), channel_id=1, replica_groups=mesh['wide_0'=2,'wide_1'=16,'wide_2'=2,'narrow'=8] {'wide_2'}, dimensions={0} | all-to-all | bytes 1310720 | tf_op jit(solution)/shard_map/all_to_all | solution.py:12
  83.9 0.9 broadcast_in_dim.22
  84.7 4.4 %all-to-all-start.4 = ((bf16[32,5,1024]{2,1,0:T(8,128)(2,1)}), bf16[32,5,1024]{2,1,0:T(8,128)(2,1)}, u32[]{:S(2)}, u32[]{:S(2)}) async-start(bf16[32,5,1024]{2,1,0:T(8,128)(2,1)} %broadcast_in_dim.22), calls=%async_computation.4 | async-start | bytes 1048576 | tf_op jit(solution)/shard_map/all_to_all | solution.py:12
  89.2 0.2 copy.63
  89.3 0.8 reshape_reshape.13
  90.2 0.4 copy.62
  90.5 0.3 reshape_reshape.12
  90.8 1.4 convolution_dynamic-update-slice_fusion.2
  92.2 1.4 convolution_dynamic-update-slice_fusion.1
  93.6 1.2 convolution_dynamic-update-slice_fusion.4
  94.8 1.1 convolution_dynamic-update-slice_fusion.3
  95.9 27.4 %all-to-all-done.4 = bf16[32,5,1024]{2,1,0:T(8,128)(2,1)} async-done(((bf16[32,5,1024]{2,1,0:T(8,128)(2,1)}), bf16[32,5,1024]{2,1,0:T(8,128)(2,1)}, u32[]{:S(2)}, u32[]{:S(2)}) %all-to-all-start.4) | async-done | bytes 327712 | tf_op jit(solution)/shard_map/all_to_all | solution.py:12
  123.3 1.3 copy.64
  124.6 0.1 broadcast_in_dim.23
  124.7 4.4 %all_to_all.48 = bf16[2,32,5,1024]{3,1,2,0:T(8,128)(2,1)S(1)} all-to-all(bf16[2,32,5,1024]{3,1,2,0:T(8,128)(2,1)S(1)} %broadcast_in_dim.23), channel_id=1, replica_groups=mesh['wide_0'=2,'wide_1'=16,'wide_2'=2,'narrow'=8] {'wide_2'}, dimensions={0} | all-to-all | bytes 1310720 | tf_op jit(solution)/shard_map/all_to_all | solution.py:12
  129.1 0.4 copy.65
  129.4 0.3 reshape_reshape.14
  129.7 1.4 convolution_dynamic-update-slice_fusion
  131.1 3.1 %copy.68 = f32[1216,448]{0,1:T(8,128)} copy(f32[1216,448]{1,0:T(8,128)} %convolution_dynamic-update-slice_fusion) | data formatting | bytes 4358144 | tf_op jit(solution)/shard_map/concatenate | solution.py:39
  134.2 4.5 %all-to-all-start.6 = ((f32[8,1216,56]{1,2,0:T(8,128)}), f32[8,1216,56]{1,2,0:T(8,128)S(1)}, u32[]{:S(2)}, u32[]{:S(2)}) async-start(f32[8,1216,56]{1,2,0:T(8,128)} %bitcast.31), calls=%async_computation.6 | async-start | bytes 4587520 | tf_op jit(solution)/shard_map/all_to_all | solution.py:34
  138.9 0.7 fusion.17
  139.6 33.5 %all-to-all-done.6 = f32[8,1216,56]{1,2,0:T(8,128)S(1)} async-done(((f32[8,1216,56]{1,2,0:T(8,128)}), f32[8,1216,56]{1,2,0:T(8,128)S(1)}, u32[]{:S(2)}, u32[]{:S(2)}) %all-to-all-start.6) | async-done | bytes 2179104 | tf_op jit(solution)/shard_map/all_to_all | solution.py:34
  173.1 0.1 reduce_sum.27
  173.3 0.1 copy.84
  173.4 1.1 gather_fusion.3
  174.5 1.1 gather_fusion.1
  175.6 0.1 copy.83
  175.6 1.1 gather_fusion
  176.7 1.1 gather_fusion.2
  177.8 1.1 gather_fusion.5
  178.9 1.1 gather_fusion.4
  180.0 1.1 gather_fusion.7
  181.1 1.1 gather_fusion.6
  182.2 0.1 copy.74
  182.3 0.1 copy.76
  182.4 0.1 copy.78
  182.5 0.1 copy.72
  182.6 0.1 copy.70
  182.8 0.1 copy.73
  182.9 0.1 copy.75
  183.0 0.1 copy.77
  183.1 5.7 %fusion.14 = bf16[56,320]{1,0:T(8,128)(2,1)S(1)} fusion(f32[1216,56]{0,1:T(8,128)S(1)} %reduce_sum.27, f32[]{:T(128)} %bitcast.5, f32[320,56]{0,1:T(8,128)S(1)} %copy.72, pred[320]{0:T(512)(128)(4,1)S(1)} %get-tuple-element.27, f32[]{:T(128)} %bitcast.6, f32[]{:T(128)} %bitcast.7, f32[]{:T(128)} %bitcast.8, f32[]{:T(128)} %bitcast.9, f32[]{:T(128)} %bitcast.10, ...), kind=kLoop, calls=%fused_computation.102 | loop fusion | flops 4193280 | bytes 467232 | tf_op jit(solution)/shard_map/transpose | solution.py:48
  188.8 0.0 copy-start.2
  188.8 6.3 %fusion.15 = bf16[56,320]{1,0:T(8,128)(2,1)S(1)} fusion(f32[320,56]{0,1:T(8,128)S(1)} %copy.77, pred[320]{0:T(512)(128)(4,1)S(1)} %get-tuple-element.24, f32[320,56]{0,1:T(8,128)S(1)} %copy.75, pred[320]{0:T(512)(128)(4,1)S(1)} %get-tuple-element.25, f32[320,56]{0,1:T(8,128)S(1)} %copy.73, pred[320]{0:T(512)(128)(4,1)S(1)} %get-tuple-element.26, ...), kind=kLoop, calls=%fused_computation.103 | loop fusion | flops 7777280 | bytes 825632 | tf_op jit(solution)/shard_map/transpose | solution.py:48
  195.2 0.1 pad_maximum_fusion
  195.3 29.4 %all_gather.3 = bf16[448,640]{1,0:T(8,128)(2,1)S(1)} all-gather(bf16[56,640]{1,0:T(8,128)(2,1)S(1)} %pad_maximum_fusion), channel_id=1, replica_groups=mesh['wide_0'=2,'wide_1'=16,'wide_2'=2,'narrow'=8] {'narrow'}, dimensions={0}, use_global_device_ids=true | all-gather | bytes 645120 | tf_op jit(solution)/shard_map/all_gather | solution.py:51
  224.6 0.5 fusion.1
  225.2 1.8 convolution_add_fusion
  226.9 1.4 reshape_reshape.15
  228.3 0.8 copy.79
  229.1 4.8 %all_to_all.49 = f32[2,32,5,1024]{3,1,2,0:T(8,128)S(1)} all-to-all(f32[2,32,5,1024]{3,1,2,0:T(8,128)S(1)} %copy.79), channel_id=1, replica_groups=mesh['wide_0'=2,'wide_1'=16,'wide_2'=2,'narrow'=8] {'wide_2'}, dimensions={0} | all-to-all | bytes 2621440 | tf_op jit(solution)/shard_map/all_to_all | solution.py:34
  233.9 0.1 reduce_sum.28
  234.0 0.4 copy.80
  234.4 61.0 %all_to_all.50 = f32[32,5,1024]{2,1,0:T(8,128)S(1)} all-to-all(f32[32,5,1024]{2,1,0:T(8,128)S(1)} %copy.80), channel_id=1, replica_groups=mesh['wide_0'=2,'wide_1'=16,'wide_2'=2,'narrow'=8] {'wide_0','wide_1'}, dimensions={0} | all-to-all | bytes 1310720 | tf_op jit(solution)/shard_map/all_to_all | solution.py:64
  295.5 0.7 reduce_sum.29
  (26 shorter events, 0.1 us)
Async XLA Ops:
  0.0 90.8 %copy-start = (bf16[1024,448]{0,1:T(8,128)(2,1)S(1)}, bf16[1024,448]{0,1:T(8,128)(2,1)}, u32[]{:S(2)}) copy-start(bf16[1024,448]{0,1:T(8,128)(2,1)} %param.12) | copy-start | bytes 2752516
  36.8 47.1 %copy-start.5 = (bf16[5,1024]{1,0:T(8,128)(2,1)S(1)}, bf16[5,1024]{1,0:T(8,128)(2,1)}, u32[]{:S(2)}) copy-start(bf16[5,1024]{1,0:T(8,128)(2,1)} %param.15) | copy-start | bytes 30724
  74.6 5.0 %all-to-all-start.3 = ((bf16[2,32,2,1024]{3,2,1,0:T(2,128)(2,1)}), bf16[2,32,2,1024]{3,2,1,0:T(2,128)(2,1)S(1)}, u32[]{:S(2)}, u32[]{:S(2)}) async-start(bf16[2,32,2,1024]{3,2,1,0:T(2,128)(2,1)} %broadcast_in_dim.21), calls=%async_computation.3 | async-start | bytes 524288 | tf_op jit(solution)/shard_map/all_to_all | solution.py:12
  84.7 38.6 %all-to-all-start.4 = ((bf16[32,5,1024]{2,1,0:T(8,128)(2,1)}), bf16[32,5,1024]{2,1,0:T(8,128)(2,1)}, u32[]{:S(2)}, u32[]{:S(2)}) async-start(bf16[32,5,1024]{2,1,0:T(8,128)(2,1)} %broadcast_in_dim.22), calls=%async_computation.4 | async-start | bytes 1048576 | tf_op jit(solution)/shard_map/all_to_all | solution.py:12
  90.2 2.1 copy-start.1
  90.8 2.8 copy-start.3
  124.6 5.1 %copy-start.4 = (bf16[448,1024]{1,0:T(8,128)(2,1)S(1)}, bf16[448,1024]{1,0:T(8,128)(2,1)}, u32[]{:S(2)}) copy-start(bf16[448,1024]{1,0:T(8,128)(2,1)} %param.14) | copy-start | bytes 2752516
  134.2 4.6 %copy-start.6 = (s32[320,4]{0,1:T(4,128)S(1)}, s32[320,4]{0,1:T(4,128)}, u32[]{:S(2)}) copy-start(s32[320,4]{0,1:T(4,128)} %param.16) | copy-start | bytes 15364
  134.2 4.7 %copy-start.7 = (s32[8]{0:T(128)S(1)}, s32[8]{0:T(128)}, u32[]{:S(2)}) copy-start(s32[8]{0:T(128)} %param.17) | copy-start | bytes 100
  134.2 38.9 %all-to-all-start.6 = ((f32[8,1216,56]{1,2,0:T(8,128)}), f32[8,1216,56]{1,2,0:T(8,128)S(1)}, u32[]{:S(2)}, u32[]{:S(2)}) async-start(f32[8,1216,56]{1,2,0:T(8,128)} %bitcast.31), calls=%async_computation.6 | async-start | bytes 4587520 | tf_op jit(solution)/shard_map/all_to_all | solution.py:34
  188.8 36.3 %copy-start.2 = (bf16[1024,448]{0,1:T(8,128)(2,1)S(1)}, bf16[1024,448]{0,1:T(8,128)(2,1)}, u32[]{:S(2)}) copy-start(bf16[1024,448]{0,1:T(8,128)(2,1)} %param.13) | copy-start | bytes 2752516
where the time goes:
time: 297 us; the launch traced here: 296 us
  blocking collectives  176 us (59%)
  waiting for transfers between devices  62.2 us (21%)
  local copies, waits for them, and re-layouts  23.4 us (8%)
  other arithmetic  13.2 us (4%)
  starting transfers between devices  12.4 us (4%)
  matrix products  8.71 us (3%)
    all_to_all x4, blocking collectives, copy_for_each(): lax.all_to_all(jnp.broadcast_to(x[None], (size, *x.shape)), axis, 0, 0, t...  80.7 us
    all_to_all x1, blocking collectives, sum_in_two_steps(): return jnp.sum(lax.all_to_all(own, far, 0, 0, tiled=True), axis=0)  61 us
    all_to_all x1, waiting for transfers between devices, summed_on_arrival(): lax.all_to_all(blocks, axis, split_axis=0, concat_axis=0, tiled=True)  33.5 us
    all_gather x1, blocking collectives, turned_gather(): out = lax.all_gather(both, axis, axis=0, tiled=True)  29.4 us
    all_to_all x2, waiting for transfers between devices, copy_for_each(): lax.all_to_all(jnp.broadcast_to(x[None], (size, *x.shape)), axis, 0, 0, t...  28.7 us
    transpose x2, other arithmetic, turned_gather(): turned = [jnp.moveaxis(a, dim, 0) for a, dim in zip(arrays, dims)]  12.1 us
    all_to_all x2, starting transfers between devices, copy_for_each(): lax.all_to_all(jnp.broadcast_to(x[None], (size, *x.shape)), axis, 0, 0, t...  7.84 us
  transfers between devices with their start and end apart: 3, of which 3 were waited for; matrix products, arithmetic and copies ran while one was open for 3% of the time, Pallas kernels for 0%

commit v1 on v0

--- a/solution.py
+++ b/solution.py
@@ -48,7 +48,9 @@
     turned = [jnp.moveaxis(a, dim, 0) for a, dim in zip(arrays, dims)]
     widths = [t[0].size for t in turned]
     both = jnp.concatenate([t.reshape(-1, w) for t, w in zip(turned, widths)], axis=1)
-    out = lax.all_gather(both, axis, axis=0, tiled=True)
+    out = jnp.concatenate(
+        lax.all_to_all(jnp.stack([both] * lax.axis_size(axis)), axis, 0, 0), axis=0
+    )
     blocks = jnp.split(out, [sum(widths[:k]) for k in range(1, len(widths))], axis=1)
     return tuple(
         (

time: 297 us -> 280 us (0.943)
  blocking collectives: 176 us -> 159 us
    all_gather x1 -> x0, blocking collectives: 29.4 us -> none  [turned_gather(): out = lax.all_gather(both, axis, axis=0, tiled=True)]
    all_to_all x0 -> x1, blocking collectives: none -> 12.9 us  [turned_gather(): lax.all_to_all(jnp.stack([both] * lax.axis_size(axis)), axis, 0, 0)]
where the time goes in v1:
time: 280 us
  blocking collectives  159 us (57%)
  waiting for transfers between devices  62.2 us (22%)
  local copies, waits for them, and re-layouts  23.4 us (8%)
  other arithmetic  13.1 us (5%)
  starting transfers between devices  12.4 us (4%)
  matrix products  8.71 us (3%)
    all_to_all x4, blocking collectives, copy_for_each(): lax.all_to_all(jnp.broadcast_to(x[None], (size, *x.shape)), axis, 0, 0, t...  80.7 us
    all_to_all x1, blocking collectives, sum_in_two_steps(): return jnp.sum(lax.all_to_all(own, far, 0, 0, tiled=True), axis=0)  60.9 us
    all_to_all x1, waiting for transfers between devices, summed_on_arrival(): lax.all_to_all(blocks, axis, split_axis=0, concat_axis=0, tiled=True)  33.5 us
    all_to_all x2, waiting for transfers between devices, copy_for_each(): lax.all_to_all(jnp.broadcast_to(x[None], (size, *x.shape)), axis, 0, 0, t...  28.7 us
    all_to_all x1, blocking collectives, turned_gather(): lax.all_to_all(jnp.stack([both] * lax.axis_size(axis)), axis, 0, 0)  12.9 us
    transpose x2, other arithmetic, turned_gather(): turned = [jnp.moveaxis(a, dim, 0) for a, dim in zip(arrays, dims)]  12 us
    all_to_all x2, starting transfers between devices, copy_for_each(): lax.all_to_all(jnp.broadcast_to(x[None], (size, *x.shape)), axis, 0, 0, t...  7.84 us
  transfers between devices with their start and end apart: 3, of which 3 were waited for; matrix products, arithmetic and copies ran while one was open for 3% of the time, Pallas kernels for 0%

profile of v1, /device:TPU:32, one launch (start us, length us, event | category | flops | bytes accessed | tf_op | source)
XLA Modules:
  0.0 279.5 jit_solution(11706142127028885322)
XLA Ops:
  0.0 0.8 broadcast_in_dim.20
  0.8 35.1 %all_to_all.50 = bf16[32,2,1024]{2,1,0:T(2,128)(2,1)S(1)} all-to-all(bf16[32,2,1024]{2,1,0:T(2,128)(2,1)S(1)} %broadcast_in_dim.20), channel_id=1, replica_groups=mesh['wide_0'=2,'wide_1'=16,'wide_2'=2,'narrow'=8] {'wide_0','wide_1'}, dimensions={0} | all-to-all | bytes 262144 | tf_op jit(solution)/shard_map/all_to_all | solution.py:12
  36.0 0.8 broadcast_in_dim.18
  36.8 37.0 %all_to_all.51 = bf16[32,5,1024]{2,1,0:T(8,128)(2,1)S(1)} all-to-all(bf16[32,5,1024]{2,1,0:T(8,128)(2,1)S(1)} %broadcast_in_dim.18), channel_id=1, replica_groups=mesh['wide_0'=2,'wide_1'=16,'wide_2'=2,'narrow'=8] {'wide_0','wide_1'}, dimensions={0} | all-to-all | bytes 655360 | tf_op jit(solution)/shard_map/all_to_all | solution.py:12
  73.7 0.8 broadcast_in_dim.21
  74.6 3.4 %all-to-all-start.3 = ((bf16[2,32,2,1024]{3,2,1,0:T(2,128)(2,1)}), bf16[2,32,2,1024]{3,2,1,0:T(2,128)(2,1)S(1)}, u32[]{:S(2)}, u32[]{:S(2)}) async-start(bf16[2,32,2,1024]{3,2,1,0:T(2,128)(2,1)} %broadcast_in_dim.21), calls=%async_computation.3 | async-start | bytes 524288 | tf_op jit(solution)/shard_map/all_to_all | solution.py:12
  78.0 0.2 copy.63
  78.2 1.3 all-to-all-done.3
  79.5 0.1 broadcast_in_dim.19
  79.6 4.3 %all_to_all.52 = bf16[2,32,5,1024]{3,1,2,0:T(8,128)(2,1)S(1)} all-to-all(bf16[2,32,5,1024]{3,1,2,0:T(8,128)(2,1)S(1)} %broadcast_in_dim.19), channel_id=1, replica_groups=mesh['wide_0'=2,'wide_1'=16,'wide_2'=2,'narrow'=8] {'wide_2'}, dimensions={0} | all-to-all | bytes 1310720 | tf_op jit(solution)/shard_map/all_to_all | solution.py:12
  83.9 0.9 broadcast_in_dim.22
  84.7 4.4 %all-to-all-start.4 = ((bf16[32,5,1024]{2,1,0:T(8,128)(2,1)}), bf16[32,5,1024]{2,1,0:T(8,128)(2,1)}, u32[]{:S(2)}, u32[]{:S(2)}) async-start(bf16[32,5,1024]{2,1,0:T(8,128)(2,1)} %broadcast_in_dim.22), calls=%async_computation.4 | async-start | bytes 1048576 | tf_op jit(solution)/shard_map/all_to_all | solution.py:12
  89.2 0.2 copy.65
  89.3 0.8 reshape_reshape.13
  90.2 0.4 copy.64
  90.5 0.3 reshape_reshape.12
  90.8 1.4 convolution_dynamic-update-slice_fusion.2
  92.2 1.4 convolution_dynamic-update-slice_fusion.1
  93.6 1.2 convolution_dynamic-update-slice_fusion.4
  94.8 1.1 convolution_dynamic-update-slice_fusion.3
  95.9 27.4 %all-to-all-done.4 = bf16[32,5,1024]{2,1,0:T(8,128)(2,1)} async-done(((bf16[32,5,1024]{2,1,0:T(8,128)(2,1)}), bf16[32,5,1024]{2,1,0:T(8,128)(2,1)}, u32[]{:S(2)}, u32[]{:S(2)}) %all-to-all-start.4) | async-done | bytes 327712 | tf_op jit(solution)/shard_map/all_to_all | solution.py:12
  123.3 1.3 copy.66
  124.6 0.1 broadcast_in_dim.23
  124.7 4.4 %all_to_all.53 = bf16[2,32,5,1024]{3,1,2,0:T(8,128)(2,1)S(1)} all-to-all(bf16[2,32,5,1024]{3,1,2,0:T(8,128)(2,1)S(1)} %broadcast_in_dim.23), channel_id=1, replica_groups=mesh['wide_0'=2,'wide_1'=16,'wide_2'=2,'narrow'=8] {'wide_2'}, dimensions={0} | all-to-all | bytes 1310720 | tf_op jit(solution)/shard_map/all_to_all | solution.py:12
  129.1 0.4 copy.67
  129.4 0.3 reshape_reshape.14
  129.7 1.4 convolution_dynamic-update-slice_fusion
  131.1 3.1 %copy.70 = f32[1216,448]{0,1:T(8,128)} copy(f32[1216,448]{1,0:T(8,128)} %convolution_dynamic-update-slice_fusion) | data formatting | bytes 4358144 | tf_op jit(solution)/shard_map/concatenate | solution.py:39
  134.2 4.5 %all-to-all-start.6 = ((f32[8,1216,56]{1,2,0:T(8,128)}), f32[8,1216,56]{1,2,0:T(8,128)S(1)}, u32[]{:S(2)}, u32[]{:S(2)}) async-start(f32[8,1216,56]{1,2,0:T(8,128)} %bitcast.32), calls=%async_computation.6 | async-start | bytes 4587520 | tf_op jit(solution)/shard_map/all_to_all | solution.py:34
  138.9 0.7 fusion.17
  139.6 33.5 %all-to-all-done.6 = f32[8,1216,56]{1,2,0:T(8,128)S(1)} async-done(((f32[8,1216,56]{1,2,0:T(8,128)}), f32[8,1216,56]{1,2,0:T(8,128)S(1)}, u32[]{:S(2)}, u32[]{:S(2)}) %all-to-all-start.6) | async-done | bytes 2179104 | tf_op jit(solution)/shard_map/all_to_all | solution.py:34
  173.1 0.1 reduce_sum.27
  173.3 0.1 copy.86
  173.4 1.1 gather_fusion.3
  174.5 1.1 gather_fusion.1
  175.6 0.1 copy.85
  175.6 1.1 gather_fusion
  176.7 1.1 gather_fusion.2
  177.8 1.1 gather_fusion.5
  178.9 1.1 gather_fusion.4
  180.0 1.1 gather_fusion.7
  181.1 1.1 gather_fusion.6
  182.2 0.1 copy.76
  182.3 0.1 copy.78
  182.4 0.1 copy.80
  182.5 0.1 copy.74
  182.6 0.1 copy.72
  182.8 0.1 copy.75
  182.9 0.1 copy.77
  183.0 0.1 copy.79
  183.1 5.7 %fusion.14 = bf16[56,320]{1,0:T(8,128)(2,1)S(1)} fusion(f32[1216,56]{0,1:T(8,128)S(1)} %reduce_sum.27, f32[]{:T(128)} %bitcast.5, f32[320,56]{0,1:T(8,128)S(1)} %copy.74, pred[320]{0:T(512)(128)(4,1)S(1)} %get-tuple-element.27, f32[]{:T(128)} %bitcast.6, f32[]{:T(128)} %bitcast.7, f32[]{:T(128)} %bitcast.8, f32[]{:T(128)} %bitcast.9, f32[]{:T(128)} %bitcast.10, ...), kind=kLoop, calls=%fused_computation.102 | loop fusion | flops 4193280 | bytes 467232 | tf_op jit(solution)/shard_map/transpose | solution.py:48
  188.8 6.3 %fusion.15 = bf16[56,320]{1,0:T(8,128)(2,1)S(1)} fusion(f32[320,56]{0,1:T(8,128)S(1)} %copy.79, pred[320]{0:T(512)(128)(4,1)S(1)} %get-tuple-element.24, f32[320,56]{0,1:T(8,128)S(1)} %copy.77, pred[320]{0:T(512)(128)(4,1)S(1)} %get-tuple-element.25, f32[320,56]{0,1:T(8,128)S(1)} %copy.75, pred[320]{0:T(512)(128)(4,1)S(1)} %get-tuple-element.26, ...), kind=kLoop, calls=%fused_computation.103 | loop fusion | flops 7777280 | bytes 825632 | tf_op jit(solution)/shard_map/transpose | solution.py:48
  195.1 0.0 copy-start.2
  195.1 0.1 pad_maximum_fusion
  195.2 12.9 %all_to_all.54 = bf16[8,56,640]{2,1,0:T(8,128)(2,1)S(1)} all-to-all(bf16[8,56,640]{2,1,0:T(8,128)(2,1)S(1)} %stack.2), channel_id=1, replica_groups=mesh['wide_0'=2,'wide_1'=16,'wide_2'=2,'narrow'=8] {'narrow'}, dimensions={0} | all-to-all | bytes 1146880 | tf_op jit(solution)/shard_map/all_to_all | solution.py:52
  208.1 0.5 fusion.1
  208.7 1.7 convolution_add_fusion
  210.4 1.4 reshape_reshape.15
  211.8 0.8 copy.81
  212.6 4.8 %all_to_all.55 = f32[2,32,5,1024]{3,1,2,0:T(8,128)S(1)} all-to-all(f32[2,32,5,1024]{3,1,2,0:T(8,128)S(1)} %copy.81), channel_id=1, replica_groups=mesh['wide_0'=2,'wide_1'=16,'wide_2'=2,'narrow'=8] {'wide_2'}, dimensions={0} | all-to-all | bytes 2621440 | tf_op jit(solution)/shard_map/all_to_all | solution.py:34
  217.4 0.1 reduce_sum.28
  217.5 0.4 copy.82
  217.9 60.9 %all_to_all.56 = f32[32,5,1024]{2,1,0:T(8,128)S(1)} all-to-all(f32[32,5,1024]{2,1,0:T(8,128)S(1)} %copy.82), channel_id=1, replica_groups=mesh['wide_0'=2,'wide_1'=16,'wide_2'=2,'narrow'=8] {'wide_0','wide_1'}, dimensions={0} | all-to-all | bytes 1310720 | tf_op jit(solution)/shard_map/all_to_all | solution.py:66
  278.8 0.7 reduce_sum.29
  (27 shorter events, 0.2 us)
Async XLA Ops:
  0.0 90.8 %copy-start = (bf16[1024,448]{0,1:T(8,128)(2,1)S(1)}, bf16[1024,448]{0,1:T(8,128)(2,1)}, u32[]{:S(2)}) copy-start(bf16[1024,448]{0,1:T(8,128)(2,1)} %param.12) | copy-start | bytes 2752516
  36.8 47.1 %copy-start.5 = (bf16[5,1024]{1,0:T(8,128)(2,1)S(1)}, bf16[5,1024]{1,0:T(8,128)(2,1)}, u32[]{:S(2)}) copy-start(bf16[5,1024]{1,0:T(8,128)(2,1)} %param.15) | copy-start | bytes 30724
  74.6 5.0 %all-to-all-start.3 = ((bf16[2,32,2,1024]{3,2,1,0:T(2,128)(2,1)}), bf16[2,32,2,1024]{3,2,1,0:T(2,128)(2,1)S(1)}, u32[]{:S(2)}, u32[]{:S(2)}) async-start(bf16[2,32,2,1024]{3,2,1,0:T(2,128)(2,1)} %broadcast_in_dim.21), calls=%async_computation.3 | async-start | bytes 524288 | tf_op jit(solution)/shard_map/all_to_all | solution.py:12
  84.7 38.6 %all-to-all-start.4 = ((bf16[32,5,1024]{2,1,0:T(8,128)(2,1)}), bf16[32,5,1024]{2,1,0:T(8,128)(2,1)}, u32[]{:S(2)}, u32[]{:S(2)}) async-start(bf16[32,5,1024]{2,1,0:T(8,128)(2,1)} %broadcast_in_dim.22), calls=%async_computation.4 | async-start | bytes 1048576 | tf_op jit(solution)/shard_map/all_to_all | solution.py:12
  90.2 2.1 copy-start.1
  90.8 2.8 copy-start.3
  124.6 5.1 %copy-start.4 = (bf16[448,1024]{1,0:T(8,128)(2,1)S(1)}, bf16[448,1024]{1,0:T(8,128)(2,1)}, u32[]{:S(2)}) copy-start(bf16[448,1024]{1,0:T(8,128)(2,1)} %param.14) | copy-start | bytes 2752516
  134.2 4.6 %copy-start.6 = (s32[320,4]{0,1:T(4,128)S(1)}, s32[320,4]{0,1:T(4,128)}, u32[]{:S(2)}) copy-start(s32[320,4]{0,1:T(4,128)} %param.16) | copy-start | bytes 15364
  134.2 4.7 %copy-start.7 = (s32[8]{0:T(128)S(1)}, s32[8]{0:T(128)}, u32[]{:S(2)}) copy-start(s32[8]{0:T(128)} %param.17) | copy-start | bytes 100
  134.2 38.9 %all-to-all-start.6 = ((f32[8,1216,56]{1,2,0:T(8,128)}), f32[8,1216,56]{1,2,0:T(8,128)S(1)}, u32[]{:S(2)}, u32[]{:S(2)}) async-start(f32[8,1216,56]{1,2,0:T(8,128)} %bitcast.32), calls=%async_computation.6 | async-start | bytes 4587520 | tf_op jit(solution)/shard_map/all_to_all | solution.py:34
  195.1 13.6 %copy-start.2 = (bf16[1024,448]{0,1:T(8,128)(2,1)S(1)}, bf16[1024,448]{0,1:T(8,128)(2,1)}, u32[]{:S(2)}) copy-start(bf16[1024,448]{0,1:T(8,128)(2,1)} %param.13) | copy-start | bytes 2752516
